TPU v7x, 128 devices: a whole 4x4x4 slice. The times are simulated.
128 devices in a mesh: dap: 64 (over y_lo, x, z, core), rep: 2 (over y_hi).
Axes of the slice: x: 4, y: 4 (y_hi: 2, y_lo: 2; y = y_hi * 2 + y_lo), z: 4, core: 2. Of those that a mesh axis runs over, the one named last changes fastest.
Arguments:
- pair_map: bfloat16 [1024, 1024, 128], P('dap'), may hold values from -6 to 6
- residue_mask: int32 [1024], replicated, may hold values from 0 to 1, as said below
- gain_start: float32 [128], replicated, may hold values from 0.25 to 1.75
- proj_start: bfloat16 [4, 128, 128], P(None, None, 'rep'), may hold values from -4 to 4
- bias_start: bfloat16 [128, 4], P(None, 'rep'), may hold values from -0.5 to 0.5
- out_start: bfloat16 [128, 128], replicated, may hold values from -3 to 3
- gain_end: float32 [128], replicated, may hold values from 0.25 to 1.75
- proj_end: bfloat16 [4, 128, 128], P(None, None, 'rep'), may hold values from -4 to 4
- bias_end: bfloat16 [128, 4], P(None, 'rep'), may hold values from -0.5 to 0.5
- out_end: bfloat16 [128, 128], replicated, may hold values from -3 to 3
Outputs:
- turned_map: bfloat16 [1024, 1024, 128], P('dap')
Inputs may be any that keep to these rules, and one draw needn't show every extreme that they name: residue_mask is 1 on the first L residues and 0 on the others, for some L from 512 to 1023.
All inputs are finite; a program needn't handle non-finite values.
Results may differ from a plain program's by a relative error of at most 0.008.
The roundings to bfloat16 on the way count: a program that leaves them out, or rounds other values in their place, can miss the bound.
Values may be sent and summed in bfloat16 or wider, within the bound.
A program may use at most 128 MiB of HBM per device.

v0:
```python
import jax
import jax.numpy as jnp
from jax import lax
from jax.sharding import PartitionSpec as P

DH = 32


epsilon = 1e-05


def normalize(values_in, gain):
    floats = values_in.astype(jnp.float32)
    center = jnp.mean(floats, axis=-1, keepdims=True)
    spread = jnp.mean((floats - center) ** 2, axis=-1, keepdims=True)
    return ((floats - center) * lax.rsqrt(spread + epsilon) * gain).astype(jnp.bfloat16)


def project(normed, projection):
    parts = jnp.einsum("abc,fch->fabh", normed, projection, preferred_element_type=jnp.float32)
    queries = (parts[0] * DH ** (-0.5)).astype(jnp.bfloat16)
    key_proj = parts[1].astype(jnp.bfloat16)
    value_proj = parts[2].astype(jnp.bfloat16)
    gate_vals = jax.nn.sigmoid(parts[3])
    return (queries, key_proj, value_proj, gate_vals)


def attend(queries, key_proj, value_proj, gate_vals, bias_plane, offset, key_valid):
    local_rows = queries.shape[0]
    length = key_proj.shape[1]
    head_count = bias_plane.shape[0]
    query_count = bias_plane.shape[1]
    query_part = lax.dynamic_slice_in_dim(queries, offset, query_count, 1)
    query_heads = query_part.reshape(local_rows, query_count, head_count, DH)
    key_heads = key_proj.reshape(local_rows, length, head_count, DH)
    value_heads = value_proj.reshape(local_rows, length, head_count, DH)
    scores = jnp.einsum(
        "aqhd,akhd->ahqk", query_heads, key_heads, preferred_element_type=jnp.float32
    )
    scores = scores + bias_plane.astype(jnp.float32)[None]
    scores = jnp.where(key_valid[None, None, None, :], scores, -1000000000.0)
    highest = jnp.max(scores, axis=-1, keepdims=True)
    expo = jnp.exp(scores - highest)
    attn = (expo / jnp.sum(expo, axis=-1, keepdims=True)).astype(jnp.bfloat16)
    outputs = jnp.einsum("ahqk,akhd->aqhd", attn, value_heads, preferred_element_type=jnp.float32)
    outputs = outputs.reshape(local_rows, query_count, head_count * DH)
    gate_part = lax.dynamic_slice_in_dim(gate_vals, offset, query_count, 1)
    return (outputs * gate_part).astype(jnp.bfloat16)


def attention_fn(queries, key_proj, value_proj, gate_vals, key_valid):
    local_rows = queries.shape[0]
    width = queries.shape[2]

    def apply_piece(pieces, offset):
        query_count = pieces.shape[1]
        block_len = 64

        def one_block(number):
            section = lax.dynamic_slice_in_dim(pieces, number * block_len, block_len, 1)
            return attend(
                queries, key_proj, value_proj, gate_vals, section, number * block_len, key_valid
            )

        results = lax.map(one_block, jnp.arange(query_count // block_len))
        return jnp.transpose(results, (1, 0, 2, 3)).reshape(local_rows, query_count, width)

    return apply_piece


def finish(base_map, heads_all, out_weight, row_mask, residue_mask):
    update = jnp.einsum("abh,hc->abc", heads_all, out_weight, preferred_element_type=jnp.float32)
    keep = (row_mask[:, None] * residue_mask[None, :]).astype(jnp.float32)[:, :, None]
    return (base_map.astype(jnp.float32) + update * keep).astype(jnp.bfloat16)


def on_device(
    pair_map,
    residue_mask,
    gain_start,
    proj_start,
    bias_start,
    out_start,
    gain_end,
    proj_end,
    bias_end,
    out_end,
):
    row_count = pair_map.shape[0]
    first_row = lax.axis_index("dap") * row_count
    row_mask = lax.dynamic_slice_in_dim(residue_mask, first_row, row_count, 0)
    key_valid = residue_mask == 1
    normed_start = normalize(pair_map, gain_start)
    q_start, k_start, v_start, g_start = project(normed_start, proj_start)
    plane_start = jnp.einsum(
        "abc,ch->hab", normed_start, bias_start, preferred_element_type=jnp.float32
    ).astype(jnp.bfloat16)
    run_start = attention_fn(q_start, k_start, v_start, g_start, key_valid)
    heads_start = run_start(lax.all_gather(plane_start, "dap", axis=1, tiled=True), jnp.int32(0))
    joined_start = lax.all_gather(heads_start, "rep", axis=2, tiled=True)
    mid_map = finish(pair_map, joined_start, out_start, row_mask, residue_mask)
    swapped_local = jnp.transpose(mid_map, (1, 0, 2))
    turned = lax.all_to_all(swapped_local, "dap", split_axis=0, concat_axis=1, tiled=True)
    normed_end = normalize(turned, gain_end)
    q_end, k_end, v_end, g_end = project(normed_end, proj_end)
    run_end = attention_fn(q_end, k_end, v_end, g_end, key_valid)
    local_plane = jnp.einsum(
        "abc,ch->hab", normed_end, bias_end, preferred_element_type=jnp.float32
    ).astype(jnp.bfloat16)
    heads_end = run_end(lax.all_gather(local_plane, "dap", axis=1, tiled=True), jnp.int32(0))
    joined_end = lax.all_gather(heads_end, "rep", axis=2, tiled=True)
    return finish(turned, joined_end, out_end, row_mask, residue_mask)


def solution(mesh):
    in_specs = (
        P("dap", None, None),
        P(),
        P(),
        P(None, None, "rep"),
        P(None, "rep"),
        P(),
        P(),
        P(None, None, "rep"),
        P(None, "rep"),
        P(),
    )
    out_specs = P("dap", None, None)
    return jax.shard_map(
        on_device, mesh=mesh, in_specs=in_specs, out_specs=out_specs, check_vma=False
    )
```

profile of v0, /device:TPU:1, one launch (start us, length us, event | category | flops | bytes accessed | tf_op | source)
XLA Modules:
  0.0 1076.4 jit_solution(11963315708575165636)
XLA Ops:
  15.0 6.5 fusion.54
  21.7 8.7 fusion.65
  36.4 94.8 %all-gather.5.cloned.1.call-done = bf16[2,1024,1024]{2,0,1:T(2,128)(2,1)} async-done(((bf16[2,16,1024]{2,0,1:T(2,128)(2,1)}), bf16[2,1024,1024]{2,0,1:T(2,128)(2,1)}) %all-gather.5.cloned.1.call-update) | async-done | bytes 4194320 | tf_op jit(solution)/shard_map/all_gather | solution.py:99
  134.3 282.3 %while.20 = (s32[]{:T(128)}, bf16[16,16,64,64]{2,3,1,0:T(8,128)(2,1)}, pred[1024]{0:T(1024)(128)(4,1)S(1)}, s32[16]{0:T(128)S(1)}, bf16[16,1024,64]{1,2,0:T(8,12...) while((s32[]{:T(128)}, ...), condition=%wide.region_5.6_spmd, body=%wide.region_2.5_spmd.sunk | while | flops 281281536 | bytes 24528580 | solution.py:65
  136.8 7.9 fusion.93
  154.4 7.9 fusion.93
  172.1 7.9 fusion.93
  189.7 7.9 fusion.93
  207.4 7.9 fusion.93
  225.0 7.9 fusion.93
  242.6 7.9 fusion.93
  260.3 7.9 fusion.93
  277.9 7.9 fusion.93
  295.6 7.9 fusion.93
  313.2 7.9 fusion.93
  330.9 7.9 fusion.93
  348.5 7.9 fusion.93
  366.1 7.9 fusion.93
  383.8 7.9 fusion.93
  401.4 7.9 fusion.93
  416.5 7.7 copy.34
  424.2 6.7 reshape.141
  431.2 59.3 %all-gather.7.cloned.1.call-done = bf16[16,1024,128]{1,2,0:T(8,128)(2,1)} async-done(((bf16[16,1024,64]{1,2,0:T(8,128)(2,1)}), bf16[16,1024,128]{1,2,0:T(8,128)(2,1)}) %all-gather.7.cloned.1.call-update) | async-done | bytes 4194320 | tf_op jit(solution)/shard_map/all_gather | solution.py:100
  490.5 5.7 fusion.32
  498.9 59.4 %all_to_all.4 = bf16[1024,16,128]{2,1,0:T(8,128)(2,1)S(1)} all-to-all(bf16[1024,16,128]{2,1,0:T(8,128)(2,1)S(1)} %copy.35), channel_id=1, replica_groups=mesh['dap'=64,'rep'=2] {'dap'}, dimensions={0} | all-to-all | bytes 8388608 | tf_op jit(solution)/shard_map/all_to_all | solution.py:103
  572.2 7.6 fusion.31
  604.9 96.0 %all-gather.9.cloned.1.call-done = bf16[2,1024,1024]{2,0,1:T(2,128)(2,1)} async-done(((bf16[2,16,1024]{2,0,1:T(2,128)(2,1)}), bf16[2,1024,1024]{2,0,1:T(2,128)(2,1)}) %all-gather.9.cloned.1.call-update) | async-done | bytes 4194320 | tf_op jit(solution)/shard_map/all_gather | solution.py:110
  704.0 284.2 %while.21 = (s32[]{:T(128)}, bf16[16,16,64,64]{2,3,1,0:T(8,128)(2,1)}, pred[1024]{0:T(1024)(128)(4,1)S(1)}, s32[16]{0:T(128)S(1)}, bf16[16,1024,64]{1,2,0:T(8,12...) while((s32[]{:T(128)}, ...), condition=%wide.region_11.12_spmd, body=%wide.region_8.11_spmd.sunk | while | flops 281281536 | bytes 24528580 | solution.py:65
  706.6 7.9 fusion.98
  724.4 7.9 fusion.98
  742.1 7.9 fusion.98
  759.9 7.9 fusion.98
  777.7 7.9 fusion.98
  795.4 7.9 fusion.98
  813.2 7.9 fusion.98
  830.9 7.9 fusion.98
  848.7 7.9 fusion.98
  866.5 7.9 fusion.98
  884.2 7.9 fusion.98
  902.0 7.9 fusion.98
  919.7 7.9 fusion.98
  937.5 7.9 fusion.98
  955.3 7.9 fusion.98
  973.0 7.9 fusion.98
  988.2 7.7 copy.44
  995.8 6.5 reshape.142
  1002.4 59.6 %all-gather.11.cloned.1.call-done = bf16[16,1024,128]{1,2,0:T(8,128)(2,1)} async-done(((bf16[16,1024,64]{1,2,0:T(8,128)(2,1)}), bf16[16,1024,128]{1,2,0:T(8,128)(2,1)}) %all-gather.11.cloned.1.call-update) | async-done | bytes 4194320 | tf_op jit(solution)/shard_map/all_gather | solution.py:111
  1062.0 7.7 fusion.29
  (259 shorter events, 357.1 us)
Async XLA Ops:
  6.5 15.2 %copy-start = (bf16[4,128,64]{1,2,0:T(8,128)(2,1)S(1)}, bf16[4,128,64]{1,2,0:T(8,128)(2,1)}, u32[]{:S(2)}) copy-start(bf16[4,128,64]{1,2,0:T(8,128)(2,1)} %param.17) | copy-start | bytes 196612
  6.5 8.4 copy-start.10
  6.5 8.4 copy-start.13
  6.5 124.7 %all-gather.5.cloned.1.call-start = ((), (), s32[]{:S(2)}) async-start(), calls=%async_computation.1 | async-start | bytes 4259840 | tf_op jit(solution)/shard_map/all_gather | solution.py:99
  6.5 3.5 copy-start.2
  14.9 6.8 copy-start.9
  21.4 469.1 %all-gather.7.cloned.1.call-start = ((), (), s32[]{:S(2)}) async-start(), calls=%async_computation.2 | async-start | bytes 6291456 | tf_op jit(solution)/shard_map/all_gather | solution.py:100
  424.2 66.3 %copy-start.7 = (bf16[128,128]{1,0:T(8,128)(2,1)S(1)}, bf16[128,128]{1,0:T(8,128)(2,1)}, u32[]{:S(2)}) copy-start(bf16[128,128]{1,0:T(8,128)(2,1)} %param.19) | copy-start | bytes 98308
  431.0 270.0 %all-gather.9.cloned.1.call-start = ((), (), s32[]{:S(2)}) async-start(), calls=%async_computation.3 | async-start | bytes 4259840 | tf_op jit(solution)/shard_map/all_gather | solution.py:110
  563.6 3.2 copy-start.4
  580.8 4.2 copy-start.11
  585.0 5.5 copy-start.3
  585.0 7.6 copy-start.12
  590.6 2.0 copy-start.5
  592.6 2.1 copy-start.6
  594.5 467.5 %all-gather.11.cloned.1.call-start = ((), (), s32[]{:S(2)}) async-start(), calls=%async_computation.4 | async-start | bytes 6291456 | tf_op jit(solution)/shard_map/all_gather | solution.py:111
  995.8 66.1 %copy-start.8 = (bf16[128,128]{1,0:T(8,128)(2,1)S(1)}, bf16[128,128]{1,0:T(8,128)(2,1)}, u32[]{:S(2)}) copy-start(bf16[128,128]{1,0:T(8,128)(2,1)} %param.23) | copy-start | bytes 98308
  1062.0 7.7 copy-start.1
Sparse Core Ops, SparseCore 0:
  21.6 109.5 all-gather.4
  431.1 59.3 all-gather.6
  594.6 106.2 all-gather.8
  1002.5 59.4 all-gather.10
where the time goes:
time: 1080 us
  matrix products  456 us (42%)
  waiting for transfers between devices  310 us (29%)
  local copies, waits for them, and re-layouts  114 us (11%)
  other arithmetic  103 us (10%)
  blocking collectives  59.4 us (6%)
  loops' own time  19.8 us (2%)
  between operations  13.6 us (1%)
    sub x32, matrix products, attend(): expo = jnp.exp(scores - highest)  252 us
    dot_general x32, matrix products, attend(): jnp.einsum('ahqk,akhd->aqhd', attn, value_heads, preferred_element_type=j...  169 us
    all_gather x1, waiting for transfers between devices, on_device(): lax.all_gather(local_plane, 'dap', axis=1, tiled=True)  96 us
    all_gather x1, waiting for transfers between devices, on_device(): lax.all_gather(plane_start, 'dap', axis=1, tiled=True)  94.8 us
    dynamic_update_slice x32, other arithmetic, apply_piece(): results = lax.map(one_block, jnp.arange(query_count // block_len))  63 us
    all_gather x1, waiting for transfers between devices, on_device(): joined_end = lax.all_gather(heads_end, 'rep', axis=2, tiled=True)  59.6 us
    all_to_all x1, blocking collectives, on_device(): lax.all_to_all(swapped_local, 'dap', split_axis=0, concat_axis=1, tiled=T...  59.4 us
    all_gather x1, waiting for transfers between devices, on_device(): joined_start = lax.all_gather(heads_start, 'rep', axis=2, tiled=True)  59.3 us
  transfers between devices with their start and end apart: 4, of which 4 were waited for; matrix products, arithmetic and copies ran while one was open for 2% of the time, Pallas kernels for 0%

commit v1 on v0

v1 whole, which is shorter than its diff:
```python
import functools, math
import jax, jax.numpy as jnp
from jax import lax
from jax.experimental import pallas as pl
from jax.experimental.pallas import tpu as pltpu
from jax.sharding import PartitionSpec as P

EPS=1e-5
LOG2E=math.log2(math.e)

def attn_kernel(L_ref, pair_ref, gain_ref, w_ref, plane_ref, outw_ref, out_ref,
                bias_ref, q_ref, k_ref, va_ref, g_ref, *, QB, KG, n, heads, dh):
    i = pl.program_id(0)
    L = L_ref[0]
    row0 = L_ref[1]
    C = pair_ref.shape[2]
    W = heads*dh
    blocks, hr, _ = plane_ref.shape
    rows = hr//heads
    lane = lax.broadcasted_iota(jnp.int32, (1, W), 1)//dh

    @pl.when(i == 0)
    def _():
        valid = lax.broadcasted_iota(jnp.int32, (1, n), 1) < L
        def prep(b, c):
            piece = plane_ref[b].astype(jnp.float32)
            piece = jnp.where(valid, piece*LOG2E, -1e9)
            for h in range(heads):
                bias_ref[h, pl.ds(pl.multiple_of(b*rows, rows), rows), :] = piece[h*rows:(h+1)*rows]
            return c
        lax.fori_loop(0, blocks, prep, 0)
        for h in range(heads):
            va_ref[h, :, W:] = jnp.broadcast_to((lane == h).astype(jnp.bfloat16), (n, W))

    x = pair_ref[0].astype(jnp.float32)
    out_ref[0] = pair_ref[0]

    @pl.when(row0 + i < L)
    def _():
        center = jnp.mean(x, axis=-1, keepdims=True)
        xc = x - center
        spread = jnp.mean(xc*xc, axis=-1, keepdims=True)
        normed = (xc*lax.rsqrt(spread+EPS)*gain_ref[...]).astype(jnp.bfloat16)
        def pr(f):
            return jnp.dot(normed, w_ref[f], preferred_element_type=jnp.float32)
        q_ref[...] = (pr(0)*(dh**-0.5*LOG2E)).astype(jnp.bfloat16)
        k_ref[...] = pr(1).astype(jnp.bfloat16)
        v = pr(2).astype(jnp.bfloat16)
        for h in range(heads):
            va_ref[h, :, :W] = jnp.where(lane == h, v, jnp.zeros_like(v))
        g_ref[...] = jax.nn.sigmoid(pr(3))

        def run(nk):
            def qblock(qb, c):
                off = pl.multiple_of(qb*QB, QB)
                qq = q_ref[pl.ds(off, QB), :]
                acc = None
                for h in range(heads):
                    qh = jnp.where(lane == h, qq, jnp.zeros_like(qq))
                    s = lax.dot_general(qh, k_ref[:nk, :], (((1,), (1,)), ((), ())), preferred_element_type=jnp.float32)
                    s = s + bias_ref[h, pl.ds(off, QB), :nk]
                    m = jnp.max(s, axis=-1, keepdims=True)
                    p = jnp.exp2(s-m).astype(jnp.bfloat16)
                    o = jnp.dot(p, va_ref[h, :nk, :], preferred_element_type=jnp.float32)
                    acc = o if acc is None else acc + o
                hd = (acc[:, :W]/acc[:, W:]*g_ref[pl.ds(off, QB), :]).astype(jnp.bfloat16)
                upd = jnp.dot(hd, outw_ref[...], preferred_element_type=jnp.float32)
                base = pair_ref[0, pl.ds(off, QB), :].astype(jnp.float32)
                keep = off + lax.broadcasted_iota(jnp.int32, (QB, 1), 0) < L
                out_ref[0, pl.ds(off, QB), :] = jnp.where(keep, base+upd, base).astype(jnp.bfloat16)
                return c
            lax.fori_loop(0, (L+QB-1)//QB, qblock, 0)
        ng = n//KG
        lo = (n//2)//KG
        for t in range(max(lo, 1), ng+1):
            cond = (L+KG-1)//KG == t
            @pl.when(cond)
            def _(t=t):
                run(t*KG)

def attention(L2, pair, gain, w, plane, outw, *, QB=512, KG=128, heads=4, dh=32):
    rows, n, C = pair.shape
    W = heads*dh
    blocks, hr, _ = plane.shape
    one = pl.Buffered(1)
    full = lambda a: pl.BlockSpec(a.shape, lambda i: (0,)*a.ndim, pipeline_mode=one)
    return pl.pallas_call(
        functools.partial(attn_kernel, QB=QB, KG=KG, n=n, heads=heads, dh=dh),
        grid=(rows,),
        in_specs=[pl.BlockSpec(memory_space=pltpu.SMEM),
                  pl.BlockSpec((1, n, C), lambda i: (i, 0, 0)),
                  full(gain), full(w), full(plane), full(outw)],
        out_specs=pl.BlockSpec((1, n, C), lambda i: (i, 0, 0)),
        out_shape=jax.ShapeDtypeStruct((rows, n, C), jnp.bfloat16),
        scratch_shapes=[pltpu.VMEM((heads, n, n), jnp.float32),
                        pltpu.VMEM((n, W), jnp.bfloat16),
                        pltpu.VMEM((n, W), jnp.bfloat16),
                        pltpu.VMEM((heads, n, 2*W), jnp.bfloat16),
                        pltpu.VMEM((n, W), jnp.float32)],
        compiler_params=pltpu.CompilerParams(vmem_limit_bytes=60*2**20),
    )(L2, pair, gain, w, plane, outw)


def plane_of(pair, gain, bias_w):
    floats = pair.astype(jnp.float32)
    center = jnp.mean(floats, axis=-1, keepdims=True)
    spread = jnp.mean((floats - center) ** 2, axis=-1, keepdims=True)
    normed = ((floats - center) * lax.rsqrt(spread + EPS) * gain).astype(jnp.bfloat16)
    plane = jnp.einsum("abc,ch->hab", normed, bias_w, preferred_element_type=jnp.float32)
    heads, rows, n = plane.shape
    return plane.astype(jnp.bfloat16).reshape(heads * rows, n)


def on_device(pair_map, residue_mask, gain_start, proj_start, bias_start, out_start, gain_end, proj_end, bias_end, out_end):
    both = ("dap", "rep")
    rows = pair_map.shape[0] // lax.axis_size("rep")
    rep = lax.axis_index("rep")
    length = jnp.sum(residue_mask)
    row0 = (lax.axis_index("dap") * lax.axis_size("rep") + rep) * rows
    facts = jnp.stack([length, row0]).astype(jnp.int32)
    proj = lax.all_gather(jnp.stack([proj_start, proj_end]), "rep", axis=3, tiled=True)
    bias = lax.all_gather(jnp.stack([bias_start, bias_end]), "rep", axis=2, tiled=True)

    def module(pair, gain, w, bw, ow):
        plane = lax.all_gather(plane_of(pair, gain, bw), both, axis=0, tiled=False)
        return attention(facts, pair, gain[None, :], w, plane, ow)

    mine = lax.dynamic_slice_in_dim(pair_map, rep * rows, rows, 0)
    mid = module(mine, gain_start, proj[0], bias[0], out_start)
    turned = lax.all_to_all(jnp.transpose(mid, (1, 0, 2)), both, split_axis=0, concat_axis=1, tiled=True)
    done = module(turned, gain_end, proj[1], bias[1], out_end)
    return lax.all_gather(done, "rep", axis=0, tiled=True)


def solution(mesh):
    in_specs = (
        P("dap", None, None), P(), P(), P(None, None, "rep"), P(None, "rep"), P(),
        P(), P(None, None, "rep"), P(None, "rep"), P(),
    )
    return jax.shard_map(on_device, mesh=mesh, in_specs=in_specs, out_specs=P("dap", None, None), check_vma=False)
```

time: 1080 us -> 907 us (0.84)
  matrix products: 456 us -> 5.87 us
  waiting for transfers between devices: 310 us -> 675 us
  Pallas kernels: 0 us -> 124 us
  local copies, waits for them, and re-layouts: 114 us -> 12.4 us
  other arithmetic: 103 us -> 23.2 us
  loops' own time: 19.8 us -> 0 us
    all_gather x4 -> x3, waiting for transfers between devices: 310 us -> 675 us  [the longest x2 615 us: module(): plane = lax.all_gather(plane_of(pair, gain, bw), both, axis=0, tiled=False)]
    sub x32 -> x0, matrix products: 252 us -> none  [attend(): expo = jnp.exp(scores - highest)]
    dot_general x38 -> x2, matrix products: 204 us -> 5.87 us  [plane_of(): jnp.einsum('abc,ch->hab', normed, bias_w, preferred_element_type=jnp.floa...]
    pallas_call x0 -> x2, Pallas kernels: none -> 124 us  [attention(): pl.pallas_call(functools.partial(attn_kernel, QB=QB, KG=KG, n=n, heads=he...]
    dynamic_update_slice x32 -> x0, other arithmetic: 63 us -> none  [apply_piece(): results = lax.map(one_block, jnp.arange(query_count // block_len))]
    dynamic_slice x97 -> x0, local copies, waits for them, and re-layouts: 60.8 us -> none  [the longest x32 36.3 us: one_block(): section = lax.dynamic_slice_in_dim(pieces, number * block_len, block_len, 1)]
    all_to_all x1, blocking collectives: 59.4 us -> 37.8 us  [on_device(): lax.all_to_all(jnp.transpose(mid, (1, 0, 2)), both, split_axis=0, concat_...]
    another operation x2 -> x0, loops' own time: 19.8 us -> none  [apply_piece(): results = lax.map(one_block, jnp.arange(query_count // block_len))]
  transfers between devices with their start and end apart: 4 -> 3, of which waited for: 4 -> 3; matrix products, arithmetic and copies ran while one was open for 2% -> 1% of each run, Pallas kernels for 0% -> 0%
where the time goes in v1:
time: 907 us; the launch traced here: 903 us
  waiting for transfers between devices  675 us (74%)
  Pallas kernels  124 us (14%)
  blocking collectives  49.1 us (5%)
  other arithmetic  23.2 us (3%)
  between operations  13.5 us (1%)
  local copies, waits for them, and re-layouts  12.4 us (1%)
    all_gather x2, waiting for transfers between devices, module(): plane = lax.all_gather(plane_of(pair, gain, bw), both, axis=0, tiled=False)  615 us
    pallas_call x2, Pallas kernels, attention(): pl.pallas_call(functools.partial(attn_kernel, QB=QB, KG=KG, n=n, heads=he...  124 us
    all_gather x1, waiting for transfers between devices, on_device(): return lax.all_gather(done, 'rep', axis=0, tiled=True)  60.6 us
    all_to_all x1, blocking collectives, on_device(): lax.all_to_all(jnp.transpose(mid, (1, 0, 2)), both, split_axis=0, concat_...  37.8 us
  transfers between devices with their start and end apart: 3, of which 3 were waited for; matrix products, arithmetic and copies ran while one was open for 1% of the time, Pallas kernels for 0%

profile of v1, /device:TPU:1, one launch (start us, length us, event | category | flops | bytes accessed | tf_op | source)
XLA Modules:
  0.0 903.4 jit_solution(980268772258787692)
XLA Ops:
  6.5 0.0 copy-start.4
  6.5 0.0 all-gather.4.cloned.1.call-start
  6.5 0.7 pad_maximum_fusion.1
  7.2 5.3 all_gather.16
  12.6 2.3 convert_reduce_fusion.1
  14.9 0.0 copy-start
  14.9 0.0 copy-start.3
  15.0 0.0 copy-start.1
  15.0 0.0 copy-start.2
  15.0 2.4 fusion.7
  17.4 0.0 copy-done.4
  17.4 2.9 fusion.16
  20.3 0.7 copy.57
  21.0 0.0 all-gather.4.cloned.1.call-update
  21.0 0.0 all-gather.6.cloned.1.call-start
  21.1 0.0 copy-done.3
  21.1 0.7 reduce_sum.45
  21.8 0.0 copy-done.1
  21.8 0.0 copy-done.2
  21.8 0.1 copy_bitcast_fusion.3
  21.9 0.1 pad_maximum_fusion
  22.0 6.0 all_gather.15
  28.0 0.1 fusion.22
  28.1 0.8 copy.35
  28.9 0.0 copy-done
  28.9 1.3 pad_add_fusion.L_ref
  30.2 306.8 %all-gather.4.cloned.1.call-done.plane_ref = bf16[128,32,1024]{2,1,0:T(8,128)(2,1)} async-done(((bf16[1,32,1024]{2,1,0:T(8,128)(2,1)}), bf16[128,32,1024]{2,1,0:T(8,128)(2,1)}) %all-gather.4.cloned.1.call-update) | async-done | bytes 8388624 | tf_op jit(solution)/shard_map/all_gather | solution.py:125
  336.9 62.2 %shard_map.100 = bf16[8,1024,128]{2,1,0:T(8,128)(2,1)} custom-call(s32[2]{0:T(128)} %pad_add_fusion.L_ref, bf16[8,1024,128]{2,1,0:T(8,128)(2,1)} %copy-done, f32[1,128]{1,0:T(1,128)} %bitcast.53, bf16[4,128,128]{2,1,0:T(8,128)(2,1)} %bitcast.49, bf16[128,32,1024]{2,1,0:T(8,128)(2,1)} %all-gather.4.cloned.1.call-done.plane_ref, bf16[128,128]{1,0:T(8,128)(2,1)} %outw_ref.2), custom_call_target="tpu_custom_call" | custom-call | tf_op jit(solution)/shard_map/pallas_call | solution.py:87
  399.1 2.9 copy.30
  402.0 37.8 %all_to_all.18 = bf16[1024,8,128]{2,1,0:T(8,128)(2,1)S(1)} all-to-all(bf16[1024,8,128]{2,1,0:T(8,128)(2,1)S(1)} %copy.30), channel_id=1, replica_groups=mesh['dap'=64,'rep'=2] {'dap','rep'}, dimensions={0} | all-to-all | bytes 4194304 | tf_op jit(solution)/shard_map/all_to_all | solution.py:130
  439.8 0.0 copy-start.5
  439.8 1.2 convert_reduce_fusion
  441.0 14.4 %fusion.4 = f32[8,128,8]{2,1,0:T(8,128)S(1)} fusion(f32[8,128,8]{2,1,0:T(8,128)S(1)} %broadcast_multiply_fusion, bf16[128,8,8,128]{3,2,1,0:T(8,128)(2,1)S(1)} %bitcast.46), kind=kLoop, calls=%fused_computation.8 | loop fusion | flops 4186112 | bytes 2162688 | tf_op jit(solution)/shard_map/reduce_sum | solution.py:107
  455.4 0.1 add_rsqrt_fusion
  455.5 0.0 copy-done.5
  455.5 2.9 fusion.19
  458.4 0.7 copy.56
  459.1 0.0 all-gather.6.cloned.1.call-update
  459.1 0.0 all-gather.8.cloned.1.call-start
  459.2 0.8 copy.37
  459.9 1.7 copy_bitcast_fusion.pair_ref
  461.7 308.0 %all-gather.6.cloned.1.call-done.plane_ref = bf16[128,32,1024]{2,1,0:T(8,128)(2,1)} async-done(((bf16[1,32,1024]{2,1,0:T(8,128)(2,1)}), bf16[128,32,1024]{2,1,0:T(8,128)(2,1)}) %all-gather.6.cloned.1.call-update) | async-done | bytes 8388624 | tf_op jit(solution)/shard_map/all_gather | solution.py:125
  769.7 61.8 %shard_map.101 = bf16[8,1024,128]{2,1,0:T(8,128)(2,1)} custom-call(s32[2]{0:T(128)} %pad_add_fusion.L_ref, bf16[8,1024,128]{2,1,0:T(8,128)(2,1)} %copy_bitcast_fusion.pair_ref, f32[1,128]{1,0:T(1,128)} %bitcast.54, bf16[4,128,128]{2,1,0:T(8,128)(2,1)} %bitcast.50, bf16[128,32,1024]{2,1,0:T(8,128)(2,1)} %all-gather.6.cloned.1.call-done.plane_ref, ...), custom_call_target="tpu_custom_call" | custom-call | tf_op jit(solution)/shard_map/pallas_call | solution.py:87
  831.5 0.0 all-gather.8.cloned.1.call-update
  831.5 60.6 %all-gather.8.cloned.1.call-done = bf16[16,1024,128]{2,1,0:T(8,128)(2,1)} async-done(((bf16[8,1024,128]{2,1,0:T(8,128)(2,1)}), bf16[16,1024,128]{2,1,0:T(8,128)(2,1)}) %all-gather.8.cloned.1.call-update) | async-done | bytes 4194320 | tf_op jit(solution)/shard_map/all_gather | solution.py:132
  892.1 4.6 copy.59
  (5 shorter events, 0.1 us)
Async XLA Ops:
  6.5 10.9 %copy-start.4 = (f32[128]{0:T(128)S(1)}, f32[128]{0:T(128)}, u32[]{:S(2)}) copy-start(f32[128]{0:T(128)} %param.12) | copy-start | bytes 1540
  6.5 330.4 %all-gather.4.cloned.1.call-start = ((), (), s32[]{:S(2)}) async-start(), calls=%async_computation.1 | async-start | bytes 8454144 | tf_op jit(solution)/shard_map/all_gather | solution.py:125
  14.9 13.9 %copy-start = (bf16[8,1024,128]{2,1,0:T(8,128)(2,1)}, bf16[8,1024,128]{2,1,0:T(8,128)(2,1)S(1)}, u32[]{:S(2)}) copy-start(bf16[8,1024,128]{2,1,0:T(8,128)(2,1)S(1)} %get-tuple-element.6.pair_ref) | copy-start | bytes 6291460
  14.9 6.1 copy-start.3
  15.0 6.8 copy-start.1
  15.0 6.8 copy-start.2
  21.0 748.7 %all-gather.6.cloned.1.call-start = ((), (), s32[]{:S(2)}) async-start(), calls=%async_computation.2 | async-start | bytes 8454144 | tf_op jit(solution)/shard_map/all_gather | solution.py:125
  439.8 15.7 %copy-start.5 = (f32[128]{0:T(128)S(1)}, f32[128]{0:T(128)}, u32[]{:S(2)}) copy-start(f32[128]{0:T(128)} %param.16) | copy-start | bytes 1540
  459.1 433.0 %all-gather.8.cloned.1.call-start = ((), (), s32[]{:S(2)}) async-start(), calls=%async_computation.3 | async-start | bytes 6291456 | tf_op jit(solution)/shard_map/all_gather | solution.py:132
Sparse Core Ops, SparseCore 0:
  21.1 315.7 all-gather.3
  459.2 310.3 all-gather.5
  831.6 60.4 all-gather.7

commit v2 on v1

v2 whole, which is shorter than its diff:
```python
import functools
import math

import jax
import jax.numpy as jnp
from jax import lax
from jax.experimental import pallas as pl
from jax.experimental.pallas import tpu as pltpu
from jax.sharding import PartitionSpec as P

EPS = 1e-5
LOG2E = math.log2(math.e)
HEADS = 4
DH = 32
W = HEADS * DH
VMEM_LIMIT = 60 * 2**20
RING = 4
CORES = 2
MESH = pl.DeviceIdType.MESH


def place():
    dap, rep = lax.axis_index("dap"), lax.axis_index("rep")
    core = lax.rem(dap, CORES)
    z = lax.rem(dap // CORES, RING)
    x = lax.rem(dap // (CORES * RING), RING)
    y = rep * 2 + dap // (CORES * RING * RING)
    return {"c": core, "y": y, "x": x, "z": z}


def block_of(at):
    dap = ((lax.rem(at["y"], 2) * RING + at["x"]) * RING + at["z"]) * CORES + at["c"]
    return dap * 2 + at["y"] // 2


def device_of(at):
    dap = ((lax.rem(at["y"], 2) * RING + at["x"]) * RING + at["z"]) * CORES + at["c"]
    return {"dap": dap, "rep": at["y"] // 2}


def shifted(at, axis, by):
    size = CORES if axis == "c" else RING
    return {**at, axis: lax.rem(at[axis] + by + size, size)}


def greet(partners):
    barrier = pltpu.get_barrier_semaphore()
    for partner in partners:
        pl.semaphore_signal(barrier, inc=1, device_id=device_of(partner), device_id_type=MESH)
    pl.semaphore_wait(barrier, len(partners))


def normalize(floats, gain):
    center = jnp.mean(floats, axis=-1, keepdims=True)
    apart = floats - center
    spread = jnp.mean(apart * apart, axis=-1, keepdims=True)
    return (apart * lax.rsqrt(spread + EPS) * gain).astype(jnp.bfloat16)


ORDERS = ("xyz", "yzx", "zxy")


def gather_parts(n):
    unit = n // 8
    return ((0, 3 * unit), (3 * unit, 3 * unit), (6 * unit, 2 * unit))


def prepare_kernel(*refs, turned, n, rows):
    if turned:
        (src_ref, gain_ref, w_ref, bw_ref, gat_ref, q_out, k_out, v_out, g_out, base_out,
         own32, own, norm_ref, q_ref, k_ref, v_ref, g_ref, core_send, core_recv, send, recv, local_sem,
         inbox, base_ref, float_ref, all_send, all_recv) = refs
    else:
        (src_ref, gain_ref, w_ref, bw_ref, gat_ref, q_out, k_out, v_out, g_out,
         own32, own, norm_ref, q_ref, k_ref, v_ref, g_ref, core_send, core_recv, send, recv, local_sem) = refs
    me = place()
    mine = block_of(me)
    blocks = CORES * RING**3
    others = [shifted(me, axis, by) for axis in "xyz" for by in (1, -1)] + [shifted(me, "c", 1)]

    if turned:
        def partner(k):
            at = {"c": lax.rem(me["c"] + lax.rem(k, CORES), CORES)}
            k = k // CORES
            for axis in "zxy":
                at[axis] = lax.rem(me[axis] + lax.rem(k, RING), RING)
                k = k // RING
            return at

        barrier = pltpu.get_barrier_semaphore()

        def hail(k, carry):
            pl.semaphore_signal(barrier, inc=1, device_id=device_of(partner(k)), device_id_type=MESH)
            return carry

        lax.fori_loop(1, blocks, hail, 0)
        pl.semaphore_wait(barrier, blocks - 1)
        keep = pltpu.make_async_copy(src_ref.at[mine], inbox.at[mine], all_recv.at[mine // 16])
        keep.start()

        def post(k, carry):
            at = partner(k)
            pltpu.make_async_remote_copy(
                src_ref=src_ref.at[block_of(at)], dst_ref=inbox.at[mine], send_sem=all_send,
                recv_sem=all_recv.at[mine // 16], device_id=device_of(at), device_id_type=MESH,
            ).start()
            return carry

        lax.fori_loop(1, blocks, post, 0)
        four = 4 * rows * rows
        to = lax.broadcasted_iota(jnp.int32, (four, four), 0)
        come = lax.broadcasted_iota(jnp.int32, (four, four), 1)
        j, which, i = to // (4 * rows), (to // rows) % 4, to % rows
        turn = (come == (which * rows + i) * rows + j).astype(jnp.bfloat16)
        for group in range(blocks // 16):
            area = inbox.at[pl.ds(group * 16, 16)]
            pltpu.make_async_copy(area, area, all_recv.at[group]).wait()
            for part in range(4):
                first = group * 16 + part * 4
                piece = inbox[first:first + 4].reshape(four, -1)
                result = jnp.dot(turn, piece, preferred_element_type=jnp.float32)
                float_ref[:, first * rows:(first + 4) * rows, :] = result.reshape(rows, 4 * rows, -1)
    else:
        greet(others)

    def plane_row(i, carry):
        floats = float_ref[i] if turned else src_ref[i].astype(jnp.float32)
        normed = normalize(floats, gain_ref[...])
        norm_ref[i] = normed
        if turned:
            base_ref[i] = floats.astype(jnp.bfloat16)
        strip = lax.dot_general(bw_ref[...], normed, (((1,), (1,)), ((), ())), preferred_element_type=jnp.float32)
        for h in range(HEADS):
            own32[pl.ds(h * rows + i, 1), :] = strip[h:h + 1]
        return carry

    lax.fori_loop(0, rows, plane_row, 0)
    own[...] = own32[...].astype(jnp.bfloat16)

    started = []
    local = []
    if turned:
        copy = pltpu.make_async_copy(base_ref, base_out, local_sem.at[4 * rows + 1])
        copy.start()
        local.append(copy)
    copy = pltpu.make_async_copy(own, gat_ref.at[me["c"], me["y"], me["x"], me["z"]], local_sem.at[4 * rows])
    copy.start()
    local.append(copy)

    def project(i):
        normed = norm_ref[i]

        def part(f):
            return jnp.dot(normed, w_ref[f], preferred_element_type=jnp.float32)

        q_ref[i] = (part(0) * (DH**-0.5 * LOG2E)).astype(jnp.bfloat16)
        k_ref[i] = part(1).astype(jnp.bfloat16)
        v_ref[i] = part(2).astype(jnp.bfloat16)
        g_ref[i] = jax.nn.sigmoid(part(3))
        for number, (a, b) in enumerate(((q_ref, q_out), (k_ref, k_out), (v_ref, v_out), (g_ref, g_out))):
            copy = pltpu.make_async_copy(a.at[i], b.at[i], local_sem.at[4 * i + number])
            copy.start()
            local.append(copy)

    def view(part, marks, half=None, split=None):
        first, width = gather_parts(n)[part]
        index = [me["c"]]
        for axis in "yxz":
            mark = marks[axis]
            if axis == split:
                index.append(pl.ds(2 * half, 2))
            elif mark is None:
                index.append(slice(None))
            else:
                index.append(mark)
        lines = pl.ds(16 * half, 16) if half is not None and split is None else slice(None)
        return gat_ref.at[(*index, lines, pl.ds(first, width))]

    def push(src, dst, to, semaphores, number):
        copy = pltpu.make_async_remote_copy(
            src_ref=src, dst_ref=dst, send_sem=semaphores[0].at[number], recv_sem=semaphores[1].at[number],
            device_id=device_of(to), device_id_type=MESH,
        )
        copy.start()
        started.append(copy)
        return copy

    def share(part, number, marks):
        area = view(part, marks)
        return push(area, area, shifted(me, "c", 1), (core_send, core_recv), part * 4 + number)

    pending = {}
    shared = []
    project_next = 0
    for phase in range(3):
        marks = {}
        if phase == 1:
            local[1 if turned else 0].wait()
        for part, order in enumerate(ORDERS):
            axis = order[phase]
            marks[part] = {a: (None if a in order[:phase] else me[a]) for a in "yxz"}
            if phase > 0:
                for copy in pending[part]:
                    copy.wait_recv()
            area = view(part, marks[part])
            source = area
            if phase == 0:
                first, width = gather_parts(n)[part]
                source = own.at[:, pl.ds(first, width)]
            pending[part] = [
                push(source, area, shifted(me, axis, by), (send, recv), ((part * 3 + phase) * 2) * 2 + way)
                for way, by in enumerate((1, -1))
            ]
            if phase == 2:
                shared.append(share(part, 0, marks[part]))
        for _ in range(phase + 1):
            project(project_next)
            project_next += 1
        for part, order in enumerate(ORDERS):
            axis = order[phase]
            split = order[0] if phase > 0 else None
            back = {**marks[part], axis: shifted(me, axis, -1)[axis]}
            ahead = {**marks[part], axis: shifted(me, axis, 1)[axis]}
            later = []
            for way, (by, held) in enumerate(((1, back), (-1, ahead))):
                pending[part][way].wait_recv()
                area = view(part, held, half=way, split=split)
                later.append(push(area, area, shifted(me, axis, by), (send, recv), ((part * 3 + phase) * 2 + 1) * 2 + way))
            if phase == 2:
                shared.append(share(part, 1, back))
                shared.append(share(part, 2, ahead))
            pending[part] = later
        if phase < 2:
            project(project_next)
            project_next += 1
    while project_next < rows:
        project(project_next)
        project_next += 1
    for part, order in enumerate(ORDERS):
        for copy in pending[part]:
            copy.wait_recv()
        axis = order[2]
        far = {**{a: None for a in "yxz"}, axis: shifted(me, axis, 2)[axis]}
        shared.append(share(part, 3, far))
    for copy in shared:
        copy.wait_recv()
    for copy in started:
        copy.wait_send()
    for number, copy in enumerate(local):
        if number != (1 if turned else 0):
            copy.wait()
    if turned:
        area = src_ref.at[pl.ds(0, blocks - 1)]
        pltpu.make_async_copy(area, area, all_send).wait()


def prepare(src, gain, w, bw, *, turned, n, rows, ident):
    c = src.shape[-1]
    shape = (rows, n, W)
    out_shape = [jax.ShapeDtypeStruct((CORES, RING, RING, RING, HEADS * rows, n), jnp.bfloat16)]
    out_shape += [jax.ShapeDtypeStruct(shape, jnp.bfloat16)] * 3 + [jax.ShapeDtypeStruct(shape, jnp.float32)]
    if turned:
        out_shape.append(jax.ShapeDtypeStruct((rows, n, c), jnp.bfloat16))
    scratch = [
        pltpu.VMEM((HEADS * rows, n), jnp.float32),
        pltpu.VMEM((HEADS * rows, n), jnp.bfloat16),
        pltpu.VMEM((rows, n, c), jnp.bfloat16),
        pltpu.VMEM(shape, jnp.bfloat16),
        pltpu.VMEM(shape, jnp.bfloat16),
        pltpu.VMEM(shape, jnp.bfloat16),
        pltpu.VMEM(shape, jnp.float32),
        pltpu.SemaphoreType.DMA((12,)),
        pltpu.SemaphoreType.DMA((12,)),
        pltpu.SemaphoreType.DMA((36,)),
        pltpu.SemaphoreType.DMA((36,)),
        pltpu.SemaphoreType.DMA((4 * rows + 2,)),
    ]
    if turned:
        scratch += [
            pltpu.VMEM(src.shape, jnp.bfloat16),
            pltpu.VMEM((rows, n, c), jnp.bfloat16),
            pltpu.VMEM((rows, n, c), jnp.float32),
            pltpu.SemaphoreType.DMA,
            pltpu.SemaphoreType.DMA((8,)),
        ]
    vmem = pl.BlockSpec(memory_space=pltpu.VMEM)
    hbm = pl.BlockSpec(memory_space=pl.ANY)
    return pl.pallas_call(
        functools.partial(prepare_kernel, turned=turned, n=n, rows=rows),
        out_shape=out_shape,
        in_specs=[hbm if turned else vmem, vmem, vmem, vmem],
        out_specs=[hbm] * len(out_shape),
        scratch_shapes=scratch,
        compiler_params=pltpu.CompilerParams(
            collective_id=ident, has_side_effects=True, vmem_limit_bytes=VMEM_LIMIT
        ),
    )(src, gain, w, bw)


def attend_kernel(facts_ref, base_ref, q_ref, k_ref, v_ref, g_ref, plane_ref, outw_ref, out_ref,
                  bias_ref, va_ref, done_ref, *, n, rows, span, step, blocked):
    pair = pl.program_id(0)
    length = facts_ref[0]
    row0 = facts_ref[1]
    lane = lax.broadcasted_iota(jnp.int32, (1, W), 1) // DH

    @pl.when(pair == 0)
    def _():
        valid = lax.broadcasted_iota(jnp.int32, (1, n), 1) < length

        def unfold(t, carry):
            at = {"z": lax.rem(t, RING), "x": lax.rem(t // RING, RING),
                  "y": lax.rem(t // RING**2, RING), "c": t // RING**3}
            piece = plane_ref[t].astype(jnp.float32)
            piece = jnp.where(valid, piece * LOG2E, -1e9)
            first = pl.multiple_of(block_of(at) * rows, rows)
            for h in range(HEADS):
                bias_ref[h, pl.ds(first, rows), :] = piece[h * rows:(h + 1) * rows]
            return carry

        lax.fori_loop(0, plane_ref.shape[0], unfold, 0)
        for h in range(HEADS):
            va_ref[h, :, W:] = jnp.broadcast_to((lane == h).astype(jnp.bfloat16), (n, W))

    def one_row(i, carry):
        done_ref[i] = base_ref[i].astype(jnp.float32)

        @pl.when(row0 + pair * 2 + i < length)
        def _():
            v = v_ref[i]
            for h in range(HEADS):
                va_ref[h, :, :W] = jnp.where(lane == h, v, jnp.zeros_like(v))

            def run(keys):
                def one_span(number, inner):
                    off = pl.multiple_of(number * span, span)
                    queries = q_ref[i, pl.ds(off, span), :]
                    total = None
                    for h in range(HEADS):
                        own = jnp.where(lane == h, queries, jnp.zeros_like(queries))
                        scores = lax.dot_general(
                            own, k_ref[i, :keys, :], (((1,), (1,)), ((), ())), preferred_element_type=jnp.float32
                        )
                        scores = scores + bias_ref[h, pl.ds(off, span), :keys]
                        highest = jnp.max(scores, axis=-1, keepdims=True)
                        expo = jnp.exp2(scores - highest).astype(jnp.bfloat16)
                        part = jnp.dot(expo, va_ref[h, :keys, :], preferred_element_type=jnp.float32)
                        total = part if total is None else total + part
                    gated = total[:, :W] / total[:, W:] * g_ref[i, pl.ds(off, span), :]
                    update = jnp.dot(gated.astype(jnp.bfloat16), outw_ref[...], preferred_element_type=jnp.float32)
                    base = done_ref[i, pl.ds(off, span), :]
                    keep = off + lax.broadcasted_iota(jnp.int32, (span, 1), 0) < length
                    done_ref[i, pl.ds(off, span), :] = jnp.where(keep, base + update, base)
                    return inner

                lax.fori_loop(0, (length + span - 1) // span, one_span, 0)

            for count in range(n // 2 // step, n // step + 1):
                @pl.when((length + step - 1) // step == count)
                def _(count=count):
                    run(count * step)

        return carry

    lax.fori_loop(0, 2, one_row, 0)
    if blocked:
        both = [done_ref[i].reshape(n // rows, rows, -1) for i in range(2)]
        out_ref[...] = jnp.concatenate(both, axis=1).astype(jnp.bfloat16)
    else:
        out_ref[...] = done_ref[...].astype(jnp.bfloat16)


def attend(facts, base, q, k, v, g, plane, outw, *, blocked, span=512, step=128):
    rows, n, c = base.shape
    plane = plane.reshape(CORES * RING**3, HEADS * rows, n)
    one = pl.Buffered(1)
    full = lambda a: pl.BlockSpec(a.shape, lambda i: (0,) * a.ndim, pipeline_mode=one)
    two = pl.BlockSpec((2, n, c), lambda i: (i, 0, 0))
    if blocked:
        out_shape = (n // rows, rows * rows, c)
        out_spec = pl.BlockSpec((n // rows, 2 * rows, c), lambda i: (0, i, 0))
    else:
        out_shape, out_spec = (rows, n, c), two
    return pl.pallas_call(
        functools.partial(attend_kernel, n=n, rows=rows, span=span, step=step, blocked=blocked),
        grid=(rows // 2,),
        in_specs=[pl.BlockSpec(memory_space=pltpu.SMEM), two, two, two, two, two, full(plane), full(outw)],
        out_specs=out_spec,
        out_shape=jax.ShapeDtypeStruct(out_shape, jnp.bfloat16),
        scratch_shapes=[
            pltpu.VMEM((HEADS, n, n), jnp.float32),
            pltpu.VMEM((HEADS, n, 2 * W), jnp.bfloat16),
            pltpu.VMEM((2, n, c), jnp.float32),
        ],
        compiler_params=pltpu.CompilerParams(vmem_limit_bytes=VMEM_LIMIT),
    )(facts, base, q, k, v, g, plane, outw)


def exchange_kernel(src_ref, out_ref, mid_ref, send, recv, local_sem, *, rows):
    me = place()
    rep = lax.axis_index("rep")
    keep = pltpu.make_async_copy(src_ref, out_ref.at[pl.ds(rep * rows, rows)], local_sem)
    keep.start()
    sides = (shifted(me, "y", 1), shifted(me, "y", -1))
    greet(sides)
    first, second = [], []

    def push(src, dst, to, number):
        copy = pltpu.make_async_remote_copy(
            src_ref=src, dst_ref=dst, send_sem=send.at[number], recv_sem=recv.at[number],
            device_id=device_of(to), device_id_type=MESH,
        )
        copy.start()
        return copy

    order = [way * (rows // 2) + t for t in range(rows // 2) for way in range(2)]
    for row in order:
        first.append(push(src_ref.at[row], mid_ref.at[row], sides[row // (rows // 2)], row))
    for row, copy in zip(order, first):
        copy.wait_recv()
        target = sides[row // (rows // 2)]
        slot = (1 - target["y"] // 2) * rows + row
        second.append(push(mid_ref.at[row], out_ref.at[slot], target, rows + row))
    for copy in second:
        copy.wait_recv()
    for copy in first + second:
        copy.wait_send()
    keep.wait()


def exchange(src, ident):
    rows, n, c = src.shape
    hbm = pl.BlockSpec(memory_space=pl.ANY)
    out, _ = pl.pallas_call(
        functools.partial(exchange_kernel, rows=rows),
        out_shape=[jax.ShapeDtypeStruct((2 * rows, n, c), src.dtype), jax.ShapeDtypeStruct(src.shape, src.dtype)],
        in_specs=[hbm],
        out_specs=[hbm, hbm],
        scratch_shapes=[
            pltpu.SemaphoreType.DMA((2 * rows,)),
            pltpu.SemaphoreType.DMA((2 * rows,)),
            pltpu.SemaphoreType.DMA,
        ],
        compiler_params=pltpu.CompilerParams(collective_id=ident, has_side_effects=True, vmem_limit_bytes=VMEM_LIMIT),
    )(src)
    return out


def on_device(pair_map, residue_mask, gain_start, proj_start, bias_start, out_start, gain_end, proj_end, bias_end, out_end):
    n = pair_map.shape[1]
    rows = pair_map.shape[0] // 2
    rep = lax.axis_index("rep")
    row0 = (lax.axis_index("dap") * 2 + rep) * rows
    facts = jnp.stack([jnp.sum(residue_mask), row0]).astype(jnp.int32)
    proj = lax.all_gather(jnp.stack([proj_start, proj_end]), "rep", axis=3, tiled=True)
    bias = lax.all_gather(jnp.stack([bias_start, bias_end]), "rep", axis=2, tiled=True)
    bias = jnp.pad(jnp.transpose(bias, (0, 2, 1)), ((0, 0), (0, 16 - HEADS), (0, 0)))
    mine = lax.dynamic_slice_in_dim(pair_map, rep * rows, rows, 0)
    plane, q, k, v, g = prepare(
        mine, gain_start[None, :], proj[0], bias[0], turned=False, n=n, rows=rows, ident=0
    )
    mid = attend(facts, mine, q, k, v, g, plane, out_start, blocked=True)
    plane, q, k, v, g, base = prepare(
        mid, gain_end[None, :], proj[1], bias[1], turned=True, n=n, rows=rows, ident=1
    )
    done = attend(facts, base, q, k, v, g, plane, out_end, blocked=False)
    return exchange(done, 2)


def solution(mesh):
    in_specs = (
        P("dap", None, None), P(), P(), P(None, None, "rep"), P(None, "rep"), P(),
        P(), P(None, None, "rep"), P(None, "rep"), P(),
    )
    return jax.shard_map(on_device, mesh=mesh, in_specs=in_specs, out_specs=P("dap", None, None), check_vma=False)
```

time: 907 us -> 350 us (0.39)
  waiting for transfers between devices: 675 us -> 0 us
  Pallas kernels: 124 us -> 320 us
  blocking collectives: 49.1 us -> 11.4 us
  other arithmetic: 23.2 us -> 3.35 us
  between operations: 13.5 us -> 0.24 us
    all_gather x3 -> x0, waiting for transfers between devices: 675 us -> none  [the longest x2 615 us: module(): plane = lax.all_gather(plane_of(pair, gain, bw), both, axis=0, tiled=False)]
    pallas_call x2 -> x5, Pallas kernels: 124 us -> 320 us  [the longest x2 133 us: prepare(): pl.pallas_call(functools.partial(prepare_kernel, turned=turned, n=n, rows...]
    all_to_all x1 -> x0, blocking collectives: 37.8 us -> none  [on_device(): lax.all_to_all(jnp.transpose(mid, (1, 0, 2)), both, split_axis=0, concat_...]
    reduce_sum x5 -> x1, other arithmetic: 20.9 us -> 1.35 us  [on_device(): facts = jnp.stack([jnp.sum(residue_mask), row0]).astype(jnp.int32)]
  transfers between devices with their start and end apart: 3 -> 0, of which waited for: 3 -> 0; matrix products, arithmetic and copies ran while one was open for 1% -> 0% of each run, Pallas kernels for 0% -> 0%
where the time goes in v2:
time: 350 us; the launch traced here: 345 us
  Pallas kernels  320 us (91%)
  blocking collectives  11.4 us (3%)
  local copies, waits for them, and re-layouts  10.9 us (3%)
    pallas_call x2, Pallas kernels, prepare(): pl.pallas_call(functools.partial(prepare_kernel, turned=turned, n=n, rows...  133 us
    pallas_call x2, Pallas kernels, attend(): pl.pallas_call(functools.partial(attend_kernel, n=n, rows=rows, span=span...  121 us
    pallas_call x1, Pallas kernels, exchange(): pl.pallas_call(functools.partial(exchange_kernel, rows=rows), out_shape=[...  64.9 us

profile of v2, /device:TPU:1, one launch (start us, length us, event | category | flops | bytes accessed | tf_op | source)
XLA Modules:
  0.0 345.5 jit_solution(14040424448726764021)
XLA Ops:
  0.0 1.4 reduce_sum.9
  1.4 1.2 pad_add_fusion.facts_ref
  2.6 0.7 pad_maximum_fusion.1
  3.3 5.3 %all_gather.7 = bf16[2,128,4]{1,0,2:T(2,128)(2,1)S(1)} all-gather(bf16[2,128,2]{1,0,2:T(2,128)(2,1)S(1)} %copy.21), channel_id=1, replica_groups=mesh['dap'=64,'rep'=2] {'rep'}, dimensions={2}, use_global_device_ids=true | all-gather | bytes 3072 | tf_op jit(solution)/shard_map/all_gather | solution.py:456
  8.6 0.6 fusion.1
  9.2 1.0 copy_bitcast_fusion
  10.2 0.1 pad_maximum_fusion
  10.3 6.0 %all_gather.6 = bf16[2,4,128,128]{2,1,0,3:T(4,128)(2,1)S(1)} all-gather(bf16[2,4,128,64]{2,1,0,3:T(4,128)(2,1)S(1)} %pad_maximum_fusion), channel_id=1, replica_groups=mesh['dap'=64,'rep'=2] {'rep'}, dimensions={3}, use_global_device_ids=true | all-gather | bytes 393216 | tf_op jit(solution)/shard_map/all_gather | solution.py:455
  16.3 0.1 fusion.2
  16.4 0.8 copy.25
  17.2 0.8 copy.24
  17.9 3.1 constant_dynamic-slice_fusion.refs_0_.base_ref
  21.0 49.2 %shard_map.100 = (bf16[2,4,4,4,32,1024]{5,4,3,2,1,0:T(8,128)(2,1)}, bf16[8,1024,128]{2,1,0:T(8,128)(2,1)}, bf16[8,1024,128]{2,1,0:T(8,128)(2,1)}, bf16[8,1024,128]{2,1,0:T(8,128)(2,1)}, f32[8,1024,128]{2,1,0:T(8,128)}) custom-call(bf16[8,1024,128]{2,1,0:T(8,128)(2,1)} %constant_dynamic-slice_fusion.refs_0_.base_ref, f32[1,128]{1,0:T(1,128)} %bitcast.26, ...), custom_call_target="tpu_custom_call" | custom-call | tf_op jit(solution)/shard_map/pallas_call | solution.py:288
  70.2 60.9 %shard_map.101.refs_0_ = bf16[128,64,128]{2,1,0:T(8,128)(2,1)} custom-call(s32[2]{0:T(128)} %pad_add_fusion.facts_ref, bf16[8,1024,128]{2,1,0:T(8,128)(2,1)} %constant_dynamic-slice_fusion.refs_0_.base_ref, bf16[8,1024,128]{2,1,0:T(8,128)(2,1)} %get-tuple-element.17.q_ref, bf16[8,1024,128]{2,1,0:T(8,128)(2,1)} %get-tuple-element.18.k_ref, ...), custom_call_target="tpu_custom_call" | custom-call | tf_op jit(solution)/shard_map/pallas_call | solution.py:384
  131.1 84.3 %shard_map.102 = (bf16[2,4,4,4,32,1024]{5,4,3,2,1,0:T(8,128)(2,1)}, bf16[8,1024,128]{2,1,0:T(8,128)(2,1)}, bf16[8,1024,128]{2,1,0:T(8,128)(2,1)}, bf16[8,1024,12...) custom-call(bf16[128,64,128]{2,1,0:T(8,128)(2,1)} %shard_map.101.refs_0_, ...), custom_call_target="tpu_custom_call" | custom-call | tf_op jit(solution)/shard_map/pallas_call | solution.py:288
  215.3 60.4 %shard_map.103.src_ref = bf16[8,1024,128]{2,1,0:T(8,128)(2,1)} custom-call(s32[2]{0:T(128)} %pad_add_fusion.facts_ref, bf16[8,1024,128]{2,1,0:T(8,128)(2,1)} %get-tuple-element.22.base_ref, bf16[8,1024,128]{2,1,0:T(8,128)(2,1)} %get-tuple-element.23.q_ref, bf16[8,1024,128]{2,1,0:T(8,128)(2,1)} %get-tuple-element.24.k_ref, ...), custom_call_target="tpu_custom_call" | custom-call | tf_op jit(solution)/shard_map/pallas_call | solution.py:384
  275.8 64.9 %shard_map.104 = (bf16[16,1024,128]{2,1,0:T(8,128)(2,1)}, bf16[8,1024,128]{2,1,0:T(8,128)(2,1)}) custom-call(bf16[8,1024,128]{2,1,0:T(8,128)(2,1)} %shard_map.103.src_ref), custom_call_target="tpu_custom_call" | custom-call | tf_op jit(solution)/shard_map/pallas_call | solution.py:434
  340.7 4.6 %copy.31 = bf16[16,1024,128]{2,1,0:T(8,128)(2,1)} copy(bf16[16,1024,128]{2,1,0:T(8,128)(2,1)} %get-tuple-element.28) | data formatting | bytes 8388608
  (2 shorter events, 0.0 us)
